TPU v7x, 128 devices: a whole 4x4x4 slice. The times are simulated.
128 devices in a mesh: row: 32 (over z, x, core), col: 4 (over y).
Axes of the slice: x: 4, y: 4, z: 4, core: 2. Of those that a mesh axis runs over, the one named last changes fastest.
Arguments:
- grid_in: bfloat16 [16384, 227], P(('row', 'col')), may hold values from -6 to 6
- mesh_init: bfloat16 [40960, 512], P(('row', 'col')), may hold values from -6 to 6
- embed_first: bfloat16 [227, 512], replicated, may hold values from -0.375 to 0.375
- embed_second: bfloat16 [512, 512], replicated, may hold values from -0.25 to 0.25
- embed_gain: float32 [512], replicated, may hold values from 0.1 to 1.9
- edge_first: bfloat16 [4, 2, 512, 512], replicated, may hold values from -0.1875 to 0.1875
- edge_second: bfloat16 [4, 512, 512], replicated, may hold values from -0.25 to 0.25
- edge_gain: float32 [4, 512], replicated, may hold values from 0.1 to 1.9
- node_first: bfloat16 [4, 2, 512, 512], replicated, may hold values from -0.1875 to 0.1875
- node_second: bfloat16 [4, 512, 512], replicated, may hold values from -0.25 to 0.25
- node_gain: float32 [4, 512], replicated, may hold values from 0.1 to 1.9
- out_weight: bfloat16 [512, 227], replicated, may hold values from -0.25 to 0.25
- enc_send: int32 [128, 9, 128], P(('row', 'col')), may hold values from 0 to 127
- enc_slot: int32 [128, 768], P(('row', 'col')), may hold values from 0 to 1151, as said below
- enc_recv: int32 [128, 768], P(('row', 'col')), may hold values from 0 to 319, never falling along the last dimension, each value on 1 to 4 neighbouring positions
- proc_send: int32 [128, 9, 256], P(('row', 'col')), may hold values from 0 to 319
- proc_slot: int32 [128, 1600], P(('row', 'col')), may hold values from 0 to 4351, as said below
- proc_recv: int32 [128, 1600], P(('row', 'col')), may hold values from 0 to 319, never falling along the last dimension, each value on 1 to 10 neighbouring positions
- dec_send: int32 [128, 9, 64], P(('row', 'col')), may hold values from 0 to 319
- dec_slot: int32 [128, 384], P(('row', 'col')), may hold values from 0 to 575, as said below
- dec_recv: int32 [128, 384], P(('row', 'col')), may hold values from 0 to 127, never falling along the last dimension, each value on 1 to 6 neighbouring positions
Outputs:
- prediction: float32 [16384, 227], P(('row', 'col'))
Inputs may be any that keep to these rules, and one draw needn't show every extreme that they name: `enc_slot`: no two edges of a device share a slot; no slot names a sender band outside 0 .. 31; in the first and the last band every other slot carries an edge. `proc_slot`: values under 9 * 256 are slots as for the other lists: distinct within a device, never naming a sender band outside 0 .. 31, all others used in the first and the last band; exactly 64 edges of each device have values from 2304 on. `dec_slot`: no two edges of a device share a slot; no slot names a sender band outside 0 .. 31; in the first and the last band every other slot carries an edge. `enc_recv`: Non-decreasing along each row; every local mesh node receives 1 to 4 edges. `proc_recv`: Non-decreasing along each row; every local mesh node receives 1 to 10 edges. `dec_recv`: Non-decreasing along each row; every local grid node receives 1 to 6 edges.
All inputs are finite; a program needn't handle non-finite values.
Results may differ from a plain program's by a relative error of at most 0.014.
Values may be sent and summed in bfloat16 or wider, within the bound.
A program may use at most 128 MiB of HBM per device.

v0:
```python
import functools

import jax
import jax.numpy as jnp
from jax import lax
from jax.experimental import pallas as pl
from jax.experimental.pallas import tpu as pltpu
from jax.sharding import PartitionSpec as P

BF = jnp.bfloat16
F32 = jnp.float32
I32 = jnp.int32
MESH = pl.DeviceIdType.MESH

L = 512
CIN = 227
G = 128
N = 320
CO = 16
FAR = 64
CE, CM, CD = 128, 256, 64
EE, EM, ED = 768, 1600, 384
EMP = 1664
FIRST_FAR = 9 * CM
EPSILON = 1e-05

ORDER = (4, 1, 7, 3, 5, 0, 2, 6, 8)
PLACE = {b: k for k, b in enumerate(ORDER)}


def dot(a, b):
    return jnp.dot(a, b, preferred_element_type=F32)


def dot_nt(a, b):
    return lax.dot_general(a, b, (((1,), (1,)), ((), ())), preferred_element_type=F32)


def iota(shape, dim):
    return lax.broadcasted_iota(I32, shape, dim)


def ones_where(cond):
    return jnp.where(cond, 1.0, 0.0).astype(BF)


def silu(v):
    u = 0.5 * v
    return (u + u * jnp.tanh(u)).astype(BF)


def layer_norm(y, gain):
    average = jnp.mean(y, axis=-1, keepdims=True)
    centered = y - average
    spread = jnp.mean(centered * centered, axis=-1, keepdims=True)
    return centered * lax.rsqrt(spread + EPSILON) * gain


def slot_receivers(slot, recv, high):
    edges = slot.shape[1]
    at_high = (slot >> 7) == iota((high, edges), 0)
    code = recv + 1
    first = jnp.where(at_high, (code >> 6).astype(F32), 0.0).astype(BF)
    second = jnp.where(at_high, (code & 63).astype(F32), 0.0).astype(BF)
    at_low = ones_where((slot & 127) == iota((128, edges), 0))
    rows = dot_nt(first, at_low) * 64.0 + dot_nt(second, at_low) - 1.0
    cols = dot_nt(at_low, first) * 64.0 + dot_nt(at_low, second) - 1.0
    return rows.astype(I32), cols.astype(I32)


def body(
    nr,
    nc,
    grid_in,
    mesh_init,
    embed_first,
    embed_second,
    embed_gain,
    edge_first_any,
    edge_second_any,
    edge_gain,
    node_first_any,
    node_second_any,
    node_gain,
    out_weight,
    enc_send,
    enc_slot,
    enc_recv,
    proc_send,
    proc_slot,
    proc_recv,
    dec_send,
    dec_slot,
    dec_recv,
    out,
    ef,
    es,
    nf,
    ns,
    tab_out,
    tab_in,
    tab_t,
    far_out,
    far_in,
    slot_pad,
    recv_pad,
    slot_2d,
    enc_halo,
    enc_w,
    enc_m,
    proc_halo,
    proc_w,
    proc_m,
    far_e,
    far_m,
    gath,
    c_out,
    c_in,
    dec_out,
    dec_in,
    dec_g,
    dec_e,
    dec_m,
    grid_lat,
    lat,
    base,
    agg,
    w_sem,
    tab_ss,
    tab_rs,
    far_ss,
    far_rs,
    halo_ss,
    halo_rs,
    g_ss,
    g_rs,
    p_ss,
    p_rs,
    y_ss,
    y_rs,
    d_ss,
    d_rs,
):
    nzx = nr // 2
    r = lax.axis_index("row")
    c = lax.axis_index("col")
    core = lax.rem(r, 2)
    zx = r // 2
    up, down = lax.rem(r + 1, nr), lax.rem(r + nr - 1, nr)
    right, left = lax.rem(c + 1, nc), lax.rem(c + nc - 1, nc)
    rows_of = {-1: down, 0: r, 1: up}
    cols_of = {-1: left, 0: c, 1: right}
    partner = r + 1 - 2 * core

    def target(b):
        return (rows_of[b // 3 - 1], cols_of[b % 3 - 1])

    def peer(d):
        return (lax.rem(zx + d, nzx) * 2 + core, c)

    def mate(i):
        return (r, lax.rem(c + nc - i, nc))

    others = [b for b in range(9) if b != 4]

    barrier = pltpu.get_barrier_semaphore()
    greeted = [target(b) for b in others] + [peer(d) for d in range(1, nzx)] + [mate(2)]
    for device in greeted:
        pl.semaphore_signal(barrier, inc=1, device_id=device, device_id_type=MESH)

    weight_copies = []
    for i in range(4):
        group = []
        for j, (source, place) in enumerate(
            (
                (edge_first_any, ef),
                (edge_second_any, es),
                (node_first_any, nf),
                (node_second_any, ns),
            )
        ):
            copy = pltpu.make_async_copy(source.at[i], place.at[i], w_sem.at[i, j])
            copy.start()
            group.append(copy)
        weight_copies.append(group)

    for b in range(9):
        tab_out[b, 0:1, :] = enc_send[0, b : b + 1, :]
        tab_out[b, 1:2, :] = proc_send[0, b : b + 1, 0:128]
        tab_out[b, 2:3, :] = proc_send[0, b : b + 1, 128:256]
        tab_out[b, 3:8, :] = jnp.zeros((5, 128), I32)
    tab_in[0] = tab_out[4]

    hidden = silu(dot(grid_in[...], embed_first[...]))
    latent = layer_norm(dot(hidden, embed_second[...]), embed_gain[...]).astype(BF)
    grid_lat[...] = latent
    weight_copies[0][0].wait()
    enc_halo[0, 0:G, :] = dot(latent, ef[0, 0]).astype(BF)

    pl.semaphore_wait(barrier, len(greeted))

    tab_copies = []
    for b in others:
        k = PLACE[b]
        copy = pltpu.make_async_remote_copy(
            tab_out.at[b], tab_in.at[k], tab_ss.at[k], tab_rs.at[k],
            device_id=target(b), device_id_type=MESH,
        )
        copy.start()
        tab_copies.append(copy)

    def halo_copy(step, halo, size, src, dst):
        b = ORDER[dst]
        dr, dc = b // 3 - 1, b % 3 - 1
        if src != 0:
            dc = 0
        return pltpu.make_async_remote_copy(
            halo.at[src, pl.ds(0, size)],
            halo.at[dst, pl.ds(0, size)],
            halo_ss.at[step, dst],
            halo_rs.at[step, dst],
            device_id=(rows_of[dr], cols_of[dc]),
            device_id_type=MESH,
        )

    def halo_direct(step, halo, size):
        copies = {}
        for b in (3, 5, 1, 7):
            k = PLACE[b]
            copies[k] = halo_copy(step, halo, size, 0, k)
            copies[k].start()
        return copies

    def halo_forward(step, halo, size, copies):
        for here, onward in ((3, (0, 6)), (5, (2, 8))):
            copies[PLACE[here]].wait_recv()
            for b in onward:
                k = PLACE[b]
                copies[k] = halo_copy(step, halo, size, PLACE[here], k)
                copies[k].start()

    def slot_messages(step, halo, w, m, i, k):
        pre = dot(w[k], halo[k])
        y = dot(silu(pre), es[i])
        message = layer_norm(y, edge_gain[i : i + 1, :]).astype(BF)
        agg[...] += dot(m[k], message)

    def node_update(i, own, summed, start):
        node = start + dot(summed.astype(BF), nf[i, 1])
        update = layer_norm(dot(silu(node), ns[i]), node_gain[i : i + 1, :])
        return (own.astype(F32) + update).astype(BF)

    copies = halo_direct(0, enc_halo, G)

    receiver_part = dot(mesh_init[...], ef[0, 1]).astype(BF)
    for k in range(9):
        enc_halo[k, G : G + N, :] = receiver_part

    slot_pad[...] = jnp.full((1, EMP), -1, I32)
    recv_pad[...] = jnp.zeros((1, EMP), I32)
    slot_pad[0:1, 0:EM] = proc_slot[...]
    recv_pad[0:1, 0:EM] = proc_recv[...]
    slot_2d[...] = jnp.full((16, 128), -1, I32)
    chunks = EMP // 128
    for i in range(chunks):
        slot_2d[i : i + 1, :] = slot_pad[0:1, i * 128 : (i + 1) * 128]
    is_far = slot_2d[...] >= FIRST_FAR
    far_ones = ones_where(is_far)
    within = dot(far_ones, ones_where(iota((128, 128), 0) <= iota((128, 128), 1)))
    above = dot(ones_where(iota((16, 16), 1) < iota((16, 16), 0)), far_ones)
    rank = within + jnp.sum(above, axis=1, keepdims=True) - 1.0
    rank = jnp.where(is_far, rank.astype(I32), -1)
    picks = jnp.concatenate(
        [ones_where(rank[i : i + 1, :] == iota((FAR, 128), 0)) for i in range(chunks)], axis=1
    )
    node = jnp.maximum(slot_pad[...] - FIRST_FAR, 0)
    row_id = iota((8, EMP), 0)
    values = jnp.where(
        row_id == 0,
        node >> 6,
        jnp.where(
            row_id == 1,
            node & 63,
            jnp.where(row_id == 2, recv_pad[...] >> 6, jnp.where(row_id == 3, recv_pad[...] & 63, 0)),
        ),
    )
    values = values.astype(F32).astype(BF)
    far_cols = dot_nt(picks, values)
    far_rows = dot_nt(values, picks)
    far_node = (far_cols[:, 0:1] * 64.0 + far_cols[:, 1:2]).astype(I32)
    far_out[...] = jnp.broadcast_to(far_node, (FAR, 128))
    far_in[0] = jnp.broadcast_to(far_node, (FAR, 128))
    far_copies = []
    for i in range(1, nc):
        copy = pltpu.make_async_remote_copy(
            far_out, far_in.at[nc - i], far_ss.at[nc - i], far_rs.at[nc - i],
            device_id=mate(i), device_id_type=MESH,
        )
        copy.start()
        far_copies.append(copy)
    far_recv_col = (far_cols[:, 2:3] * 64.0 + far_cols[:, 3:4]).astype(I32)
    far_recv_row = (far_rows[2:3, :] * 64.0 + far_rows[3:4, :]).astype(I32)
    far_e[...] = ones_where(far_recv_col == iota((FAR, N), 1))
    far_m[...] = ones_where(far_recv_row == iota((N, FAR), 0))

    enc_rows, enc_cols = slot_receivers(enc_slot[...], enc_recv[...], 16)
    for copy in tab_copies:
        copy.wait_recv()
    tab_t[0:72, :] = tab_in[...].reshape(72, 128).astype(F32)
    tab_t[72:128, :] = jnp.zeros((56, 128), F32)
    tabs = jnp.transpose(tab_t[...]).astype(I32)
    for k in range(9):
        b = ORDER[k]
        at = iota((CE, G + N), 1)
        receiver = enc_cols[:, b : b + 1]
        receiver = jnp.where(receiver < 0, -1, receiver + G)
        enc_w[k] = ones_where((at == tabs[:, 8 * k : 8 * k + 1]) | (at == receiver))
        enc_m[k] = ones_where(enc_rows[b : b + 1, :] == iota((N, CE), 0))

    weight_copies[0][1].wait()
    agg[...] = jnp.zeros((N, L), F32)
    slot_messages(0, enc_halo.at[:], enc_w, enc_m, 0, 0)
    halo_forward(0, enc_halo, G, copies)
    weight_copies[0][2].wait()
    weight_copies[0][3].wait()
    base[...] = dot(mesh_init[...], nf[0, 0])

    proc_rows, proc_cols = slot_receivers(slot_pad[...], recv_pad[...], 24)
    for k in range(9):
        b = ORDER[k]
        at = iota((128, 2 * N), 1)
        for half in range(2):
            h = 2 * b + half
            receiver = proc_cols[:, h : h + 1]
            receiver = jnp.where(receiver < 0, -1, receiver + N)
            sender = tabs[:, 8 * k + 1 + half : 8 * k + 2 + half]
            span = slice(half * 128, (half + 1) * 128)
            proc_w[k, span, :] = ones_where((at == sender) | (at == receiver))
            proc_m[k, :, span] = ones_where(proc_rows[h : h + 1, :] == iota((N, 128), 0))

    dec_rows, dec_cols = slot_receivers(dec_slot[...], dec_recv[...], 16)
    for h in range(5):
        span = slice(h * 128, (h + 1) * 128)
        dec_e[span, :] = ones_where(dec_cols[:, h : h + 1] == iota((128, G), 1))
        dec_m[:, span] = ones_where(dec_rows[h : h + 1, :] == iota((G, 128), 0))
    tab_t[...] = jnp.zeros((128, 128), F32)
    tab_t[0:9, 0:CD] = dec_send[0].astype(F32)
    dec_tabs = jnp.transpose(tab_t[...]).astype(I32)
    for b in range(9):
        dec_g[b * CD : (b + 1) * CD, :] = ones_where(dec_tabs[0:CD, b : b + 1] == iota((CD, N), 1))
    dec_in[9 * CD : 640, :] = jnp.zeros((64, L), BF)

    @pl.loop(1, 3)
    def _(k):
        halo_wait(0, enc_halo, G, halo_rs, k)
        slot_messages(0, enc_halo, enc_w, enc_m, 0, k)

    @pl.loop(3, 5)
    def _(k):
        slot_messages(0, enc_halo, enc_w, enc_m, 0, k)

    @pl.loop(5, 9)
    def _(k):
        halo_wait(0, enc_halo, G, halo_rs, k)
        slot_messages(0, enc_halo, enc_w, enc_m, 0, k)

    lat[...] = node_update(0, mesh_init[...], agg[...], base[...])
    for copy in copies.values():
        copy.wait_send()
    for copy in tab_copies + far_copies:
        copy.wait_send()

    for s in range(2):
        i = s + 1
        halo = proc_halo.at[s]
        for copy in weight_copies[i]:
            copy.wait()
        own = lat[...]
        sent = dot(own, ef[i, 0]).astype(BF)
        halo[0, 0:N, :] = sent
        copies = halo_direct(i, halo, N)
        place = pl.multiple_of((core * nzx + zx) * CO, CO)
        gath[s, pl.ds(place, CO), :] = sent[0:CO, :]
        peer_copies = []
        for d in range(1, nzx):
            copy = pltpu.make_async_remote_copy(
                gath.at[s, pl.ds(place, CO)], gath.at[s, pl.ds(place, CO)],
                g_ss.at[s, d], g_rs.at[s, d], device_id=peer(d), device_id_type=MESH,
            )
            copy.start()
            peer_copies.append(copy)
        receiver_part = dot(own, ef[i, 1]).astype(BF)
        for k in range(9):
            halo[k, N : 2 * N, :] = receiver_part
        agg[...] = jnp.zeros((N, L), F32)
        slot_messages(i, halo, proc_w, proc_m, i, 0)
        halo_forward(i, halo, N, copies)

        for copy in peer_copies:
            copy.wait_recv()
        mine = pl.ds(pl.multiple_of(core * (nzx * CO), CO), nzx * CO)
        to_partner = pltpu.make_async_remote_copy(
            gath.at[s, mine], gath.at[s, mine], p_ss.at[s], p_rs.at[s],
            device_id=(partner, c), device_id_type=MESH,
        )
        to_partner.start()
        base[...] = dot(own, nf[i, 0])

        @pl.loop(1, 3)
        def _(k):
            halo_wait(i, halo, N, halo_rs, k)
            slot_messages(i, halo, proc_w, proc_m, i, k)

        to_partner.wait_recv()
        if s == 0:
            for copy in far_copies:
                copy.wait_recv()
        found = []
        for q in range(nc):
            number = far_in[q]
            device = number // CO
            band = device // nc
            index = (band % 2) * (nzx * CO) + (band // 2) * CO + number % CO
            index = jnp.where(device % nc == c, index, -1)
            found.append(
                jnp.concatenate(
                    [ones_where(index == iota((FAR, 128), 1) + 128 * t) for t in range(nr * CO // 128)],
                    axis=1,
                )
            )
        chosen = dot(jnp.concatenate(found, axis=0), gath[s]).astype(BF)
        c_out[s] = chosen
        mate_copies = []
        for q in range(1, nc):
            copy = pltpu.make_async_remote_copy(
                c_out.at[s, pl.ds(q * FAR, FAR)], c_in.at[s, q], y_ss.at[s, q], y_rs.at[s, q],
                device_id=mate(q), device_id_type=MESH,
            )
            copy.start()
            mate_copies.append(copy)

        @pl.loop(3, 5)
        def _(k):
            slot_messages(i, halo, proc_w, proc_m, i, k)

        @pl.loop(5, 9)
        def _(k):
            halo_wait(i, halo, N, halo_rs, k)
            slot_messages(i, halo, proc_w, proc_m, i, k)

        pre = c_out[s, 0:FAR, :].astype(F32) + dot(far_e[...], halo[0, N : 2 * N, :])
        for copy in mate_copies:
            copy.wait_recv()
        for q in range(1, nc):
            pre = pre + c_in[s, q].astype(F32)
        y = dot(silu(pre), es[i])
        message = layer_norm(y, edge_gain[i : i + 1, :]).astype(BF)
        summed = agg[...] + dot(far_m[...], message)
        lat[...] = node_update(i, own, summed, base[...])
        for copy in list(copies.values()) + peer_copies + mate_copies + [to_partner]:
            copy.wait_send()

    for copy in weight_copies[3]:
        copy.wait()
    sent = dot(lat[...], ef[3, 0]).astype(BF)
    dec_out[...] = dot(dec_g[...], sent).astype(BF)
    dec_copies = []
    for b in others:
        span = pl.ds(b * CD, CD)
        copy = pltpu.make_async_remote_copy(
            dec_out.at[span], dec_in.at[span], d_ss.at[b], d_rs.at[b],
            device_id=target(b), device_id_type=MESH,
        )
        copy.start()
        dec_copies.append(copy)
    dec_in[4 * CD : 5 * CD, :] = dec_out[4 * CD : 5 * CD, :]
    own = grid_lat[...]
    receiver_part = dot(own, ef[3, 1]).astype(BF)
    near = dot(dec_e[...], receiver_part)
    start = dot(own, nf[3, 0])
    for copy in dec_copies:
        copy.wait_recv()
    pre = dec_in[...].astype(F32) + near
    y = dot(silu(pre), es[3])
    message = layer_norm(y, edge_gain[3:4, :]).astype(BF)
    final = node_update(3, own, dot(dec_m[...], message), start)
    out[...] = grid_in[...].astype(F32) + dot(final, out_weight[...])
    for copy in dec_copies:
        copy.wait_send()


def halo_wait(step, halo, size, sems, k):
    pltpu.make_async_copy(halo.at[k, pl.ds(0, size)], halo.at[k, pl.ds(0, size)], sems.at[step, k]).wait()


def on_device(nr, nc, *args):
    vmem = pl.BlockSpec(memory_space=pltpu.VMEM)
    hbm = pl.BlockSpec(memory_space=pl.ANY)
    in_specs = [vmem] * 21
    for at in (5, 6, 8, 9):
        in_specs[at] = hbm
    args = list(args)
    args[4] = args[4].reshape(1, L)
    dma = pltpu.SemaphoreType.DMA
    nzx = nr // 2
    return pl.pallas_call(
        functools.partial(body, nr, nc),
        out_shape=jax.ShapeDtypeStruct((G, CIN), F32),
        in_specs=in_specs,
        out_specs=vmem,
        scratch_shapes=[
            pltpu.VMEM((4, 2, L, L), BF),
            pltpu.VMEM((4, L, L), BF),
            pltpu.VMEM((4, 2, L, L), BF),
            pltpu.VMEM((4, L, L), BF),
            pltpu.VMEM((9, 8, 128), I32),
            pltpu.VMEM((9, 8, 128), I32),
            pltpu.VMEM((128, 128), F32),
            pltpu.VMEM((FAR, 128), I32),
            pltpu.VMEM((nc, FAR, 128), I32),
            pltpu.VMEM((1, EMP), I32),
            pltpu.VMEM((1, EMP), I32),
            pltpu.VMEM((16, 128), I32),
            pltpu.VMEM((9, G + N, L), BF),
            pltpu.VMEM((9, CE, G + N), BF),
            pltpu.VMEM((9, N, CE), BF),
            pltpu.VMEM((2, 9, 2 * N, L), BF),
            pltpu.VMEM((9, CM, 2 * N), BF),
            pltpu.VMEM((9, N, CM), BF),
            pltpu.VMEM((FAR, N), BF),
            pltpu.VMEM((N, FAR), BF),
            pltpu.VMEM((2, nr * CO, L), BF),
            pltpu.VMEM((2, nc * FAR, L), BF),
            pltpu.VMEM((2, nc, FAR, L), BF),
            pltpu.VMEM((9 * CD, L), BF),
            pltpu.VMEM((640, L), BF),
            pltpu.VMEM((9 * CD, N), BF),
            pltpu.VMEM((640, G), BF),
            pltpu.VMEM((G, 640), BF),
            pltpu.VMEM((G, L), BF),
            pltpu.VMEM((N, L), BF),
            pltpu.VMEM((N, L), F32),
            pltpu.VMEM((N, L), F32),
            dma((4, 4)),
            dma((9,)),
            dma((9,)),
            dma((nc,)),
            dma((nc,)),
            dma((3, 9)),
            dma((3, 9)),
            dma((2, nzx)),
            dma((2, nzx)),
            dma((2,)),
            dma((2,)),
            dma((2, nc)),
            dma((2, nc)),
            dma((9,)),
            dma((9,)),
        ],
        compiler_params=pltpu.CompilerParams(
            collective_id=0, has_side_effects=True, vmem_limit_bytes=60 * 1024 * 1024
        ),
    )(*args)


def solution(mesh):
    both = ("row", "col")
    placed = (
        (P(both, None),) * 2
        + (P(),) * 10
        + (P(both, None, None), P(both, None), P(both, None)) * 3
    )
    return jax.shard_map(
        functools.partial(on_device, mesh.shape["row"], mesh.shape["col"]),
        mesh=mesh,
        in_specs=placed,
        out_specs=P(both, None),
        check_vma=False,
    )
```

profile of v0, /device:TPU:0, one launch (start us, length us, event | category | flops | bytes accessed | tf_op | source)
XLA Modules:
  0.0 93.1 jit_solution(16253965072384470016)
XLA Ops:
  0.0 1.3 %copy.24.enc_send = s32[1,9,128]{2,1,0:T(8,128)} copy(s32[1,9,128]{2,0,1:T(1,128)} %param.33) | data formatting | bytes 9216 | tf_op args[12]
  1.3 1.3 %copy.26.dec_send = s32[1,9,64]{2,1,0:T(8,128)} copy(s32[1,9,64]{2,0,1:T(1,128)} %param.39) | data formatting | bytes 4608 | tf_op args[18]
  2.6 1.3 %copy.25.proc_send = s32[1,9,256]{2,1,0:T(8,128)} copy(s32[1,9,256]{2,0,1:T(1,128)} %param.36) | data formatting | bytes 18432 | tf_op args[15]
  3.9 1.6 %copy.22.grid_in = bf16[128,227]{1,0:T(8,128)(2,1)} copy(bf16[128,227]{0,1:T(8,128)(2,1)} %param.21) | data formatting | bytes 116224 | tf_op args[0]
  5.4 1.8 %copy.23.out_weight = bf16[512,227]{1,0:T(8,128)(2,1)} copy(bf16[512,227]{0,1:T(8,128)(2,1)} %param.32) | data formatting | bytes 464896 | tf_op args[11]
  7.2 84.3 %shard_map.199 = f32[128,227]{1,0:T(8,128)} custom-call(bf16[128,227]{1,0:T(8,128)(2,1)} %copy.22.grid_in, bf16[320,512]{1,0:T(8,128)(2,1)} %mesh_init.1, bf16[227,512]{1,0:T(8,128)(2,1)} %embed_first.1, bf16[512,512]{1,0:T(8,128)(2,1)} %embed_second.1, f32[1,512]{1,0:T(1,128)} %bitcast.1, bf16[4,2,512,512]{3,2,1,0:T(8,128)(2,1)} %edge_first_any.1, ...), custom_call_target="tpu_custom_call" | custom-call | tf_op jit(solution)/shard_map/pallas_call | solution.py:506
  91.5 1.7 %copy.27 = f32[128,227]{0,1:T(8,128)} copy(f32[128,227]{1,0:T(8,128)} %shard_map.199) | data formatting | bytes 232448 | tf_op jit(solution)/shard_map/pallas_call | solution.py:506
where the time goes:
time: 93.5 us; the launch traced here: 93.1 us
  Pallas kernels  84.3 us (90%)
  local copies, waits for them, and re-layouts  8.84 us (9%)
    pallas_call x1, Pallas kernels, on_device(): pl.pallas_call(functools.partial(body, nr, nc), out_shape=jax.ShapeDtypeS...  84.3 us
    unnamed x5, local copies, waits for them, and re-layouts  7.19 us

commit v1 on v0

--- a/solution.py
+++ b/solution.py
@@ -24,8 +24,7 @@
 FIRST_FAR = 9 * CM
 EPSILON = 1e-05
 
-ORDER = (4, 1, 7, 3, 5, 0, 2, 6, 8)
-PLACE = {b: k for k, b in enumerate(ORDER)}
+CH = 80
 
 
 def dot(a, b):
@@ -97,6 +96,8 @@
     es,
     nf,
     ns,
+    mesh_own,
+    out_own,
     tab_out,
     tab_in,
     tab_t,
@@ -112,7 +113,6 @@
     proc_w,
     proc_m,
     far_e,
-    far_m,
     gath,
     c_out,
     c_in,
@@ -125,6 +125,7 @@
     lat,
     base,
     agg,
+    msg,
     w_sem,
     tab_ss,
     tab_rs,
@@ -162,6 +163,9 @@
         return (r, lax.rem(c + nc - i, nc))
 
     others = [b for b in range(9) if b != 4]
+    first_core = core == 0
+    x_row = r - 1 + 2 * core
+    x_row = lax.rem(x_row + nr, nr)
 
     barrier = pltpu.get_barrier_semaphore()
     greeted = [target(b) for b in others] + [peer(d) for d in range(1, nzx)] + [mate(2)]
@@ -183,15 +187,24 @@
             copy.start()
             group.append(copy)
         weight_copies.append(group)
+        if i == 0:
+            mesh_copies = [pltpu.make_async_copy(mesh_init, mesh_own, w_sem.at[4, 0])]
+            mesh_copies[0].start()
+    out_copy = pltpu.make_async_copy(out_weight, out_own, w_sem.at[4, 1])
+    out_copy.start()
 
     for b in range(9):
-        tab_out[b, 0:1, :] = enc_send[0, b : b + 1, :]
-        tab_out[b, 1:2, :] = proc_send[0, b : b + 1, 0:128]
-        tab_out[b, 2:3, :] = proc_send[0, b : b + 1, 128:256]
+        tab_out[b, 0:1, :] = enc_send[b]
+        tab_out[b, 1:2, :] = proc_send[b, :, 0:128]
+        tab_out[b, 2:3, :] = proc_send[b, :, 128:256]
         tab_out[b, 3:8, :] = jnp.zeros((5, 128), I32)
     tab_in[0] = tab_out[4]
 
-    hidden = silu(dot(grid_in[...], embed_first[...]))
+    hidden = silu(
+        lax.dot_general(
+            grid_in[...], embed_first[...], (((0,), (0,)), ((), ())), preferred_element_type=F32
+        )
+    )
     latent = layer_norm(dot(hidden, embed_second[...]), embed_gain[...]).astype(BF)
     grid_lat[...] = latent
     weight_copies[0][0].wait()
@@ -199,60 +212,71 @@
 
     pl.semaphore_wait(barrier, len(greeted))
 
+    toward_partner = 4 + 3 * (1 - 2 * core)
+    toward_x = 4 - 3 * (1 - 2 * core)
     tab_copies = []
-    for b in others:
-        k = PLACE[b]
+    for place, block, device in (
+        (1, toward_partner, (partner, c)),
+        (2, 3, (r, left)),
+        (3, 5, (r, right)),
+        (4, toward_x, (x_row, c)),
+        (5, toward_partner - 1, (partner, left)),
+        (6, toward_partner + 1, (partner, right)),
+        (7, toward_x - 1, (x_row, left)),
+        (8, toward_x + 1, (x_row, right)),
+    ):
         copy = pltpu.make_async_remote_copy(
-            tab_out.at[b], tab_in.at[k], tab_ss.at[k], tab_rs.at[k],
-            device_id=target(b), device_id_type=MESH,
+            tab_out.at[block], tab_in.at[place], tab_ss.at[place], tab_rs.at[place],
+            device_id=device, device_id_type=MESH,
         )
         copy.start()
         tab_copies.append(copy)
 
-    def halo_copy(step, halo, size, src, dst):
-        b = ORDER[dst]
-        dr, dc = b // 3 - 1, b % 3 - 1
-        if src != 0:
-            dc = 0
-        return pltpu.make_async_remote_copy(
-            halo.at[src, pl.ds(0, size)],
-            halo.at[dst, pl.ds(0, size)],
-            halo_ss.at[step, dst],
-            halo_rs.at[step, dst],
-            device_id=(rows_of[dr], cols_of[dc]),
-            device_id_type=MESH,
+    def send(step, halo, src, dst, first, count, piece, device, started):
+        span = pl.ds(first, count)
+        copy = pltpu.make_async_remote_copy(
+            halo.at[src, span], halo.at[dst, span],
+            halo_ss.at[step, dst, piece], halo_rs.at[step, dst, piece],
+            device_id=device, device_id_type=MESH,
         )
-
-    def halo_direct(step, halo, size):
-        copies = {}
-        for b in (3, 5, 1, 7):
-            k = PLACE[b]
-            copies[k] = halo_copy(step, halo, size, 0, k)
-            copies[k].start()
-        return copies
-
-    def halo_forward(step, halo, size, copies):
-        for here, onward in ((3, (0, 6)), (5, (2, 8))):
-            copies[PLACE[here]].wait_recv()
-            for b in onward:
-                k = PLACE[b]
-                copies[k] = halo_copy(step, halo, size, PLACE[here], k)
-                copies[k].start()
-
-    def slot_messages(step, halo, w, m, i, k):
-        pre = dot(w[k], halo[k])
-        y = dot(silu(pre), es[i])
-        message = layer_norm(y, edge_gain[i : i + 1, :]).astype(BF)
-        agg[...] += dot(m[k], message)
+        copy.start()
+        started.append(copy)
+
+    def arrived(step, halo, place, first, count, piece):
+        rows = halo.at[place, pl.ds(first, count)]
+        pltpu.make_async_copy(rows, rows, halo_rs.at[step, place, piece]).wait()
+
+    def messages(halo, w, size, i, places, msg, extra=None):
+        hidden = [silu(dot(w[k], halo[k])) for k in places]
+        if extra is not None:
+            hidden.append(silu(extra))
+        y = dot(jnp.concatenate(hidden, axis=0), es[i])
+        first = places[0] * size
+        msg[first : first + y.shape[0], :] = layer_norm(y, edge_gain[i : i + 1, :]).astype(BF)
 
     def node_update(i, own, summed, start):
         node = start + dot(summed.astype(BF), nf[i, 1])
         update = layer_norm(dot(silu(node), ns[i]), node_gain[i : i + 1, :])
         return (own.astype(F32) + update).astype(BF)
 
-    copies = halo_direct(0, enc_halo, G)
-
-    receiver_part = dot(mesh_init[...], ef[0, 1]).astype(BF)
+    def blocks_at(place):
+        return ((4, 4), (1, 7), (3, 3), (5, 5), (7, 1), (0, 6), (2, 8), (6, 0), (8, 2))[place]
+
+    def pick(place, take):
+        one, two = blocks_at(place)
+        return take(one) if one == two else jnp.where(first_core, take(one), take(two))
+
+    started = []
+    send(0, enc_halo, 0, 3, 0, G, 0, (r, right), started)
+    send(0, enc_halo, 0, 2, 0, G, 0, (r, left), started)
+    send(0, enc_halo, 0, 8, 0, G, 0, (x_row, right), started)
+    send(0, enc_halo, 0, 7, 0, G, 0, (x_row, left), started)
+    send(0, enc_halo, 0, 4, 0, G, 0, (x_row, c), started)
+    send(0, enc_halo, 0, 1, 0, G, 0, (partner, c), started)
+
+    for copy in mesh_copies:
+        copy.wait()
+    receiver_part = dot(mesh_own[...], ef[0, 1]).astype(BF)
     for k in range(9):
         enc_halo[k, G : G + N, :] = receiver_part
 
@@ -301,7 +325,7 @@
     far_recv_col = (far_cols[:, 2:3] * 64.0 + far_cols[:, 3:4]).astype(I32)
     far_recv_row = (far_rows[2:3, :] * 64.0 + far_rows[3:4, :]).astype(I32)
     far_e[...] = ones_where(far_recv_col == iota((FAR, N), 1))
-    far_m[...] = ones_where(far_recv_row == iota((N, FAR), 0))
+    proc_m[:, 9 * CM :] = ones_where(far_recv_row == iota((N, FAR), 0))
 
     enc_rows, enc_cols = slot_receivers(enc_slot[...], enc_recv[...], 16)
     for copy in tab_copies:
@@ -310,33 +334,37 @@
     tab_t[72:128, :] = jnp.zeros((56, 128), F32)
     tabs = jnp.transpose(tab_t[...]).astype(I32)
     for k in range(9):
-        b = ORDER[k]
         at = iota((CE, G + N), 1)
-        receiver = enc_cols[:, b : b + 1]
+        receiver = pick(k, lambda b: enc_cols[:, b : b + 1])
         receiver = jnp.where(receiver < 0, -1, receiver + G)
         enc_w[k] = ones_where((at == tabs[:, 8 * k : 8 * k + 1]) | (at == receiver))
-        enc_m[k] = ones_where(enc_rows[b : b + 1, :] == iota((N, CE), 0))
+        receiver = pick(k, lambda b: enc_rows[b : b + 1, :])
+        enc_m[:, k * CE : (k + 1) * CE] = ones_where(receiver == iota((N, CE), 0))
 
     weight_copies[0][1].wait()
-    agg[...] = jnp.zeros((N, L), F32)
-    slot_messages(0, enc_halo.at[:], enc_w, enc_m, 0, 0)
-    halo_forward(0, enc_halo, G, copies)
+    messages(enc_halo, enc_w, CE, 0, (0,), msg)
+    arrived(0, enc_halo, 2, 0, G, 0)
+    send(0, enc_halo, 2, 5, 0, G, 0, (partner, c), started)
+    arrived(0, enc_halo, 3, 0, G, 0)
+    send(0, enc_halo, 3, 6, 0, G, 0, (partner, c), started)
     weight_copies[0][2].wait()
     weight_copies[0][3].wait()
-    base[...] = dot(mesh_init[...], nf[0, 0])
+    base[...] = dot(mesh_own[...], nf[0, 0])
+    arrived(0, enc_halo, 1, 0, G, 0)
+    messages(enc_halo, enc_w, CE, 0, (1, 2, 3), msg)
 
     proc_rows, proc_cols = slot_receivers(slot_pad[...], recv_pad[...], 24)
     for k in range(9):
-        b = ORDER[k]
         at = iota((128, 2 * N), 1)
         for half in range(2):
-            h = 2 * b + half
-            receiver = proc_cols[:, h : h + 1]
+            receiver = pick(k, lambda b: proc_cols[:, 2 * b + half : 2 * b + half + 1])
             receiver = jnp.where(receiver < 0, -1, receiver + N)
             sender = tabs[:, 8 * k + 1 + half : 8 * k + 2 + half]
             span = slice(half * 128, (half + 1) * 128)
             proc_w[k, span, :] = ones_where((at == sender) | (at == receiver))
-            proc_m[k, :, span] = ones_where(proc_rows[h : h + 1, :] == iota((N, 128), 0))
+            receiver = pick(k, lambda b: proc_rows[2 * b + half : 2 * b + half + 1, :])
+            first = k * CM + half * 128
+            proc_m[:, first : first + 128] = ones_where(receiver == iota((N, 128), 0))
 
     dec_rows, dec_cols = slot_receivers(dec_slot[...], dec_recv[...], 16)
     for h in range(5):
@@ -344,30 +372,23 @@
         dec_e[span, :] = ones_where(dec_cols[:, h : h + 1] == iota((128, G), 1))
         dec_m[:, span] = ones_where(dec_rows[h : h + 1, :] == iota((G, 128), 0))
     tab_t[...] = jnp.zeros((128, 128), F32)
-    tab_t[0:9, 0:CD] = dec_send[0].astype(F32)
+    for b in range(9):
+        tab_t[b : b + 1, 0:CD] = dec_send[b].astype(F32)
     dec_tabs = jnp.transpose(tab_t[...]).astype(I32)
     for b in range(9):
         dec_g[b * CD : (b + 1) * CD, :] = ones_where(dec_tabs[0:CD, b : b + 1] == iota((CD, N), 1))
     dec_in[9 * CD : 640, :] = jnp.zeros((64, L), BF)
 
-    @pl.loop(1, 3)
-    def _(k):
-        halo_wait(0, enc_halo, G, halo_rs, k)
-        slot_messages(0, enc_halo, enc_w, enc_m, 0, k)
-
-    @pl.loop(3, 5)
-    def _(k):
-        slot_messages(0, enc_halo, enc_w, enc_m, 0, k)
-
-    @pl.loop(5, 9)
-    def _(k):
-        halo_wait(0, enc_halo, G, halo_rs, k)
-        slot_messages(0, enc_halo, enc_w, enc_m, 0, k)
-
-    lat[...] = node_update(0, mesh_init[...], agg[...], base[...])
-    for copy in copies.values():
-        copy.wait_send()
-    for copy in tab_copies + far_copies:
+    for k in (4, 5, 6):
+        arrived(0, enc_halo, k, 0, G, 0)
+    messages(enc_halo, enc_w, CE, 0, (4, 5, 6), msg)
+    agg[...] = dot(enc_m[:, 0 : 7 * CE], msg[0 : 7 * CE, :])
+    for k in (7, 8):
+        arrived(0, enc_halo, k, 0, G, 0)
+    messages(enc_halo, enc_w, CE, 0, (7, 8), msg)
+    summed = agg[...] + dot(enc_m[:, 7 * CE : 9 * CE], msg[7 * CE : 9 * CE, :])
+    lat[...] = node_update(0, mesh_own[...], summed, base[...])
+    for copy in started + tab_copies + far_copies:
         copy.wait_send()
 
     for s in range(2):
@@ -378,7 +399,6 @@
         own = lat[...]
         sent = dot(own, ef[i, 0]).astype(BF)
         halo[0, 0:N, :] = sent
-        copies = halo_direct(i, halo, N)
         place = pl.multiple_of((core * nzx + zx) * CO, CO)
         gath[s, pl.ds(place, CO), :] = sent[0:CO, :]
         peer_copies = []
@@ -389,13 +409,33 @@
             )
             copy.start()
             peer_copies.append(copy)
+        started = []
+        for piece in range(4):
+            send(i, halo, 0, 3, piece * CH, CH, piece, (r, right), started)
+            send(i, halo, 0, 2, piece * CH, CH, piece, (r, left), started)
+            if piece == 0:
+                send(i, halo, 0, 4, 3 * CH, CH, 3, (x_row, c), started)
+                send(i, halo, 0, 4, 0, 3 * CH, 0, (x_row, c), started)
+                send(i, halo, 0, 1, 0, N, 0, (partner, c), started)
         receiver_part = dot(own, ef[i, 1]).astype(BF)
         for k in range(9):
             halo[k, N : 2 * N, :] = receiver_part
-        agg[...] = jnp.zeros((N, L), F32)
-        slot_messages(i, halo, proc_w, proc_m, i, 0)
-        halo_forward(i, halo, N, copies)
-
+        base[...] = dot(own, nf[i, 0])
+        arrived(i, halo, 1, 0, N, 0)
+        messages(halo, proc_w, CM, i, (0, 1), msg)
+        for piece in range(3):
+            arrived(i, halo, 2, piece * CH, CH, piece)
+            send(i, halo, 2, 7, piece * CH, CH, piece, (x_row, c), started)
+            arrived(i, halo, 3, piece * CH, CH, piece)
+            send(i, halo, 3, 8, piece * CH, CH, piece, (x_row, c), started)
+            if piece == 0:
+                arrived(i, halo, 4, 3 * CH, CH, 3)
+                send(i, halo, 4, 8, 3 * CH, CH, 3, (r, right), started)
+                send(i, halo, 4, 7, 3 * CH, CH, 3, (r, left), started)
+        arrived(i, halo, 2, 3 * CH, CH, 3)
+        send(i, halo, 2, 5, 0, N, 0, (partner, c), started)
+        arrived(i, halo, 3, 3 * CH, CH, 3)
+        send(i, halo, 3, 6, 0, N, 0, (partner, c), started)
         for copy in peer_copies:
             copy.wait_recv()
         mine = pl.ds(pl.multiple_of(core * (nzx * CO), CO), nzx * CO)
@@ -404,12 +444,7 @@
             device_id=(partner, c), device_id_type=MESH,
         )
         to_partner.start()
-        base[...] = dot(own, nf[i, 0])
-
-        @pl.loop(1, 3)
-        def _(k):
-            halo_wait(i, halo, N, halo_rs, k)
-            slot_messages(i, halo, proc_w, proc_m, i, k)
+        messages(halo, proc_w, CM, i, (2, 3), msg)
 
         to_partner.wait_recv()
         if s == 0:
@@ -424,7 +459,7 @@
             index = jnp.where(device % nc == c, index, -1)
             found.append(
                 jnp.concatenate(
-                    [ones_where(index == iota((FAR, 128), 1) + 128 * t) for t in range(nr * CO // 128)],
+                    [ones_where(index == iota((FAR, 128), 1) + 128 * t) for t in range(max(1, nr * CO // 128))],
                     axis=1,
                 )
             )
@@ -439,25 +474,23 @@
             copy.start()
             mate_copies.append(copy)
 
-        @pl.loop(3, 5)
-        def _(k):
-            slot_messages(i, halo, proc_w, proc_m, i, k)
-
-        @pl.loop(5, 9)
-        def _(k):
-            halo_wait(i, halo, N, halo_rs, k)
-            slot_messages(i, halo, proc_w, proc_m, i, k)
-
+        arrived(i, halo, 4, 0, 3 * CH, 0)
+        for k in (5, 6):
+            arrived(i, halo, k, 0, N, 0)
+        messages(halo, proc_w, CM, i, (4, 5, 6), msg)
+        agg[...] = dot(proc_m[:, 0 : 7 * CM], msg[0 : 7 * CM, :])
         pre = c_out[s, 0:FAR, :].astype(F32) + dot(far_e[...], halo[0, N : 2 * N, :])
         for copy in mate_copies:
             copy.wait_recv()
         for q in range(1, nc):
             pre = pre + c_in[s, q].astype(F32)
-        y = dot(silu(pre), es[i])
-        message = layer_norm(y, edge_gain[i : i + 1, :]).astype(BF)
-        summed = agg[...] + dot(far_m[...], message)
+        for k in (7, 8):
+            for piece in range(4):
+                arrived(i, halo, k, piece * CH, CH, piece)
+        messages(halo, proc_w, CM, i, (7, 8), msg, pre)
+        summed = agg[...] + dot(proc_m[:, 7 * CM :], msg[7 * CM :, :])
         lat[...] = node_update(i, own, summed, base[...])
-        for copy in list(copies.values()) + peer_copies + mate_copies + [to_partner]:
+        for copy in started + peer_copies + mate_copies + [to_partner]:
             copy.wait_send()
 
     for copy in weight_copies[3]:
@@ -483,29 +516,30 @@
     pre = dec_in[...].astype(F32) + near
     y = dot(silu(pre), es[3])
     message = layer_norm(y, edge_gain[3:4, :]).astype(BF)
+    out_copy.wait()
     final = node_update(3, own, dot(dec_m[...], message), start)
-    out[...] = grid_in[...].astype(F32) + dot(final, out_weight[...])
+    out[...] = grid_in[...].astype(F32) + dot_nt(out_own[...], final)
     for copy in dec_copies:
         copy.wait_send()
-
-
-def halo_wait(step, halo, size, sems, k):
-    pltpu.make_async_copy(halo.at[k, pl.ds(0, size)], halo.at[k, pl.ds(0, size)], sems.at[step, k]).wait()
 
 
 def on_device(nr, nc, *args):
     vmem = pl.BlockSpec(memory_space=pltpu.VMEM)
     hbm = pl.BlockSpec(memory_space=pl.ANY)
     in_specs = [vmem] * 21
-    for at in (5, 6, 8, 9):
+    for at in (1, 5, 6, 8, 9, 11):
         in_specs[at] = hbm
     args = list(args)
     args[4] = args[4].reshape(1, L)
+    args[0] = args[0].T
+    args[11] = args[11].T
+    for at in (12, 15, 18):
+        args[at] = jnp.transpose(args[at], (1, 0, 2))
     dma = pltpu.SemaphoreType.DMA
     nzx = nr // 2
-    return pl.pallas_call(
+    prediction = pl.pallas_call(
         functools.partial(body, nr, nc),
-        out_shape=jax.ShapeDtypeStruct((G, CIN), F32),
+        out_shape=jax.ShapeDtypeStruct((CIN, G), F32),
         in_specs=in_specs,
         out_specs=vmem,
         scratch_shapes=[
@@ -513,6 +547,8 @@
             pltpu.VMEM((4, L, L), BF),
             pltpu.VMEM((4, 2, L, L), BF),
             pltpu.VMEM((4, L, L), BF),
+            pltpu.VMEM((N, L), BF),
+            pltpu.VMEM((CIN, L), BF),
             pltpu.VMEM((9, 8, 128), I32),
             pltpu.VMEM((9, 8, 128), I32),
             pltpu.VMEM((128, 128), F32),
@@ -523,12 +559,11 @@
             pltpu.VMEM((16, 128), I32),
             pltpu.VMEM((9, G + N, L), BF),
             pltpu.VMEM((9, CE, G + N), BF),
-            pltpu.VMEM((9, N, CE), BF),
+            pltpu.VMEM((N, 9 * CE), BF),
             pltpu.VMEM((2, 9, 2 * N, L), BF),
             pltpu.VMEM((9, CM, 2 * N), BF),
-            pltpu.VMEM((9, N, CM), BF),
+            pltpu.VMEM((N, 9 * CM + FAR), BF),
             pltpu.VMEM((FAR, N), BF),
-            pltpu.VMEM((N, FAR), BF),
             pltpu.VMEM((2, nr * CO, L), BF),
             pltpu.VMEM((2, nc * FAR, L), BF),
             pltpu.VMEM((2, nc, FAR, L), BF),
@@ -541,13 +576,14 @@
             pltpu.VMEM((N, L), BF),
             pltpu.VMEM((N, L), F32),
             pltpu.VMEM((N, L), F32),
-            dma((4, 4)),
+            pltpu.VMEM((9 * CM + FAR, L), BF),
+            dma((5, 4)),
             dma((9,)),
             dma((9,)),
             dma((nc,)),
             dma((nc,)),
-            dma((3, 9)),
-            dma((3, 9)),
+            dma((3, 9, 4)),
+            dma((3, 9, 4)),
             dma((2, nzx)),
             dma((2, nzx)),
             dma((2,)),
@@ -561,6 +597,7 @@
             collective_id=0, has_side_effects=True, vmem_limit_bytes=60 * 1024 * 1024
         ),
     )(*args)
+    return prediction.T
 
 
 def solution(mesh):

time: 93.5 us -> 79.3 us (0.85)
  the two profiles are of different devices: /device:TPU:0 before, /device:TPU:1 now
where the time goes in v1:
time: 79.3 us; the launch traced here: 79.1 us
  Pallas kernels  77.6 us (98%)
  local copies, waits for them, and re-layouts  1.56 us (2%)
    pallas_call x1, Pallas kernels, on_device(): pl.pallas_call(functools.partial(body, nr, nc), out_shape=jax.ShapeDtypeS...  77.6 us

profile of v1, /device:TPU:1, one launch (start us, length us, event | category | flops | bytes accessed | tf_op | source)
XLA Modules:
  0.0 79.1 jit_solution(2172391878282840860)
XLA Ops:
  0.0 77.6 %shard_map.199 = f32[227,128]{1,0:T(8,128)} custom-call(bf16[227,128]{1,0:T(8,128)(2,1)} %bitcast.9, bf16[320,512]{1,0:T(8,128)(2,1)} %mesh_init.1, bf16[227,512]{1,0:T(8,128)(2,1)} %embed_first.1, bf16[512,512]{1,0:T(8,128)(2,1)} %embed_second.1, f32[1,512]{1,0:T(1,128)} %bitcast.13, bf16[4,2,512,512]{3,2,1,0:T(8,128)(2,1)} %edge_first_any.1, ...), custom_call_target="tpu_custom_call" | custom-call | tf_op jit(solution)/shard_map/pallas_call | solution.py:540
  77.6 1.6 %copy.23 = f32[128,227]{0,1:T(8,128)} copy(f32[128,227]{0,1:T(8,128)} %bitcast.7) | data formatting | bytes 232448

commit v2 on v1

--- a/solution.py
+++ b/solution.py
@@ -24,7 +24,10 @@
 FIRST_FAR = 9 * CM
 EPSILON = 1e-05
 
+PIECES = ((0, 64), (64, 64), (128, 128), (256, 64))
+LAST = len(PIECES) - 1
 CH = 80
+GRID_PIECES = ((0, 64), (64, 64))
 
 
 def dot(a, b):
@@ -70,28 +73,43 @@
 def body(
     nr,
     nc,
+    grid_in_any,
+    mesh_init,
+    embed_first_any,
+    embed_second_any,
+    embed_gain_any,
+    edge_first_any,
+    edge_second_any,
+    edge_gain_any,
+    node_first_any,
+    node_second_any,
+    node_gain_any,
+    out_weight,
+    enc_send_any,
+    enc_slot_any,
+    enc_recv_any,
+    proc_send_any,
+    proc_slot_any,
+    proc_recv_any,
+    dec_send_any,
+    dec_slot_any,
+    dec_recv_any,
+    out,
+    enc_send,
+    proc_send,
     grid_in,
-    mesh_init,
     embed_first,
     embed_second,
     embed_gain,
-    edge_first_any,
-    edge_second_any,
-    edge_gain,
-    node_first_any,
-    node_second_any,
-    node_gain,
-    out_weight,
-    enc_send,
+    proc_slot,
+    proc_recv,
     enc_slot,
     enc_recv,
-    proc_send,
-    proc_slot,
-    proc_recv,
+    edge_gain,
+    node_gain,
     dec_send,
     dec_slot,
     dec_recv,
-    out,
     ef,
     es,
     nf,
@@ -100,9 +118,12 @@
     out_own,
     tab_out,
     tab_in,
+    tab_side,
     tab_t,
+    tab_cols,
     far_out,
     far_in,
+    far_pick,
     slot_pad,
     recv_pad,
     slot_2d,
@@ -127,6 +148,7 @@
     agg,
     msg,
     w_sem,
+    in_sem,
     tab_ss,
     tab_rs,
     far_ss,
@@ -168,9 +190,34 @@
     x_row = lax.rem(x_row + nr, nr)
 
     barrier = pltpu.get_barrier_semaphore()
-    greeted = [target(b) for b in others] + [peer(d) for d in range(1, nzx)] + [mate(2)]
+    greeted = [(x_row, c)] + [peer(d) for d in range(1, nzx)]
+    greeted += [mate(2), (r, left), (r, right), (partner, c)]
     for device in greeted:
         pl.semaphore_signal(barrier, inc=1, device_id=device, device_id_type=MESH)
+
+    loads = []
+    for at, (source, place) in enumerate(
+        (
+            (enc_send_any, enc_send),
+            (proc_send_any, proc_send),
+            (grid_in_any, grid_in),
+            (embed_first_any, embed_first),
+            (embed_second_any, embed_second),
+            (embed_gain_any, embed_gain),
+            (proc_slot_any, proc_slot),
+            (proc_recv_any, proc_recv),
+            (enc_slot_any, enc_slot),
+            (enc_recv_any, enc_recv),
+            (edge_gain_any, edge_gain),
+            (node_gain_any, node_gain),
+            (dec_send_any, dec_send),
+            (dec_slot_any, dec_slot),
+            (dec_recv_any, dec_recv),
+        )
+    ):
+        copy = pltpu.make_async_copy(source, place, in_sem.at[at])
+        copy.start()
+        loads.append(copy)
 
     weight_copies = []
     for i in range(4):
@@ -184,21 +231,29 @@
             )
         ):
             copy = pltpu.make_async_copy(source.at[i], place.at[i], w_sem.at[i, j])
-            copy.start()
             group.append(copy)
+            if i == 0:
+                copy.start()
         weight_copies.append(group)
         if i == 0:
             mesh_copies = [pltpu.make_async_copy(mesh_init, mesh_own, w_sem.at[4, 0])]
             mesh_copies[0].start()
     out_copy = pltpu.make_async_copy(out_weight, out_own, w_sem.at[4, 1])
-    out_copy.start()
-
-    for b in range(9):
-        tab_out[b, 0:1, :] = enc_send[b]
-        tab_out[b, 1:2, :] = proc_send[b, :, 0:128]
-        tab_out[b, 2:3, :] = proc_send[b, :, 128:256]
-        tab_out[b, 3:8, :] = jnp.zeros((5, 128), I32)
-    tab_in[0] = tab_out[4]
+
+    for copy in loads:
+        copy.wait()
+
+    toward_partner = 4 + 3 * (1 - 2 * core)
+    toward_x = 4 - 3 * (1 - 2 * core)
+    for at, b in enumerate(
+        (4, toward_partner, toward_x)
+        + (5, toward_partner + 1, toward_x + 1)
+        + (3, toward_partner - 1, toward_x - 1)
+    ):
+        tab_out[at, 0:1, :] = enc_send[b]
+        tab_out[at, 1:2, :] = proc_send[b, :, 0:128]
+        tab_out[at, 2:3, :] = proc_send[b, :, 128:256]
+        tab_out[at, 3:8, :] = jnp.zeros((5, 128), I32)
 
     hidden = silu(
         lax.dot_general(
@@ -212,22 +267,11 @@
 
     pl.semaphore_wait(barrier, len(greeted))
 
-    toward_partner = 4 + 3 * (1 - 2 * core)
-    toward_x = 4 - 3 * (1 - 2 * core)
     tab_copies = []
-    for place, block, device in (
-        (1, toward_partner, (partner, c)),
-        (2, 3, (r, left)),
-        (3, 5, (r, right)),
-        (4, toward_x, (x_row, c)),
-        (5, toward_partner - 1, (partner, left)),
-        (6, toward_partner + 1, (partner, right)),
-        (7, toward_x - 1, (x_row, left)),
-        (8, toward_x + 1, (x_row, right)),
-    ):
+
+    def send_tab(source, place, at, device):
         copy = pltpu.make_async_remote_copy(
-            tab_out.at[block], tab_in.at[place], tab_ss.at[place], tab_rs.at[place],
-            device_id=device, device_id_type=MESH,
+            source, place, tab_ss.at[at], tab_rs.at[at], device_id=device, device_id_type=MESH
         )
         copy.start()
         tab_copies.append(copy)
@@ -259,6 +303,45 @@
         update = layer_norm(dot(silu(node), ns[i]), node_gain[i : i + 1, :])
         return (own.astype(F32) + update).astype(BF)
 
+    def begin_step(i, first, count, latents, started, pushes):
+        s = i - 1
+        halo = proc_halo.at[s]
+        sent = dot(latents, ef[i, 0]).astype(BF)
+        halo[0, first : first + count, :] = sent
+        if first == 0:
+            place = pl.ds(pl.multiple_of((core * nzx + zx) * CO, CO), CO)
+            gath[s, place, :] = sent[0:CO, :]
+            for d in range(1, nzx):
+                copy = pltpu.make_async_remote_copy(
+                    gath.at[s, place], gath.at[s, place],
+                    g_ss.at[s, d], g_rs.at[s, d], device_id=peer(d), device_id_type=MESH,
+                )
+                copy.start()
+                pushes.append(copy)
+            pieces = (0,)
+        else:
+            send(i, halo, 0, 4, 3 * CH, CH, 3, (x_row, c), started)
+            send(i, halo, 0, 4, 0, 3 * CH, 0, (x_row, c), started)
+            send(i, halo, 0, 1, 0, N, 0, (partner, c), started)
+            pieces = (1, 2, 3)
+        for piece in pieces:
+            send(i, halo, 0, 3, piece * CH, CH, piece, (r, right), started)
+            send(i, halo, 0, 2, piece * CH, CH, piece, (r, left), started)
+
+    def finish_step(i, own, m, first, last):
+        started, pushes = [], []
+        if i < 2:
+            for copy in weight_copies[i + 1]:
+                copy.wait()
+        for at, count in ((0, CH), (CH, N - CH)):
+            part = slice(at, at + count)
+            summed = agg[part, :] + dot(m[part, first:last], msg[first:last, :])
+            latents = node_update(i, own[part, :], summed, base[part, :])
+            lat[part, :] = latents
+            if i < 2:
+                begin_step(i + 1, at, count, latents, started, pushes)
+        return started, pushes
+
     def blocks_at(place):
         return ((4, 4), (1, 7), (3, 3), (5, 5), (7, 1), (0, 6), (2, 8), (6, 0), (8, 2))[place]
 
@@ -267,12 +350,16 @@
         return take(one) if one == two else jnp.where(first_core, take(one), take(two))
 
     started = []
-    send(0, enc_halo, 0, 3, 0, G, 0, (r, right), started)
-    send(0, enc_halo, 0, 2, 0, G, 0, (r, left), started)
-    send(0, enc_halo, 0, 8, 0, G, 0, (x_row, right), started)
-    send(0, enc_halo, 0, 7, 0, G, 0, (x_row, left), started)
-    send(0, enc_halo, 0, 4, 0, G, 0, (x_row, c), started)
-    send(0, enc_halo, 0, 1, 0, G, 0, (partner, c), started)
+    send_tab(tab_out.at[pl.ds(3, 3)], tab_side.at[1], 3, (r, right))
+    send_tab(tab_out.at[pl.ds(6, 3)], tab_side.at[0], 2, (r, left))
+    send_tab(tab_out.at[1], tab_in.at[1], 1, (partner, c))
+    send_tab(tab_out.at[2], tab_in.at[4], 4, (x_row, c))
+    for piece, (first, count) in enumerate(GRID_PIECES):
+        send(0, enc_halo, 0, 3, first, count, piece, (r, right), started)
+        send(0, enc_halo, 0, 2, first, count, piece, (r, left), started)
+        if piece == 0:
+            send(0, enc_halo, 0, 4, 0, G, 0, (x_row, c), started)
+            send(0, enc_halo, 0, 1, 0, G, 0, (partner, c), started)
 
     for copy in mesh_copies:
         copy.wait()
@@ -328,95 +415,129 @@
     proc_m[:, 9 * CM :] = ones_where(far_recv_row == iota((N, FAR), 0))
 
     enc_rows, enc_cols = slot_receivers(enc_slot[...], enc_recv[...], 16)
-    for copy in tab_copies:
-        copy.wait_recv()
-    tab_t[0:72, :] = tab_in[...].reshape(72, 128).astype(F32)
-    tab_t[72:128, :] = jnp.zeros((56, 128), F32)
-    tabs = jnp.transpose(tab_t[...]).astype(I32)
     for k in range(9):
-        at = iota((CE, G + N), 1)
-        receiver = pick(k, lambda b: enc_cols[:, b : b + 1])
-        receiver = jnp.where(receiver < 0, -1, receiver + G)
-        enc_w[k] = ones_where((at == tabs[:, 8 * k : 8 * k + 1]) | (at == receiver))
         receiver = pick(k, lambda b: enc_rows[b : b + 1, :])
         enc_m[:, k * CE : (k + 1) * CE] = ones_where(receiver == iota((N, CE), 0))
 
-    weight_copies[0][1].wait()
-    messages(enc_halo, enc_w, CE, 0, (0,), msg)
-    arrived(0, enc_halo, 2, 0, G, 0)
+    def tables(places, at):
+        first, count = places[0], len(places)
+        tab_t[0 : 8 * count, :] = tab_in[first : first + count].reshape(8 * count, 128).astype(F32)
+        tab_t[8 * count :, :] = jnp.zeros((128 - 8 * count, 128), F32)
+        tab_cols[at] = jnp.transpose(tab_t[...]).astype(I32)
+
+    def enc_matrices(places, at):
+        for k in places:
+            here = iota((CE, G + N), 1)
+            receiver = pick(k, lambda b: enc_cols[:, b : b + 1])
+            receiver = jnp.where(receiver < 0, -1, receiver + G)
+            column = 8 * (k - places[0])
+            sender = tab_cols[at, :, column : column + 1]
+            enc_w[k] = ones_where((here == sender) | (here == receiver))
+
+    def proc_matrices(places, at):
+        for k in places:
+            here = iota((128, 2 * N), 1)
+            for half in range(2):
+                receiver = pick(k, lambda b: proc_cols[:, 2 * b + half : 2 * b + half + 1])
+                receiver = jnp.where(receiver < 0, -1, receiver + N)
+                column = 8 * (k - places[0]) + 1 + half
+                sender = tab_cols[at, :, column : column + 1]
+                span = slice(half * 128, (half + 1) * 128)
+                proc_w[k, span, :] = ones_where((here == sender) | (here == receiver))
+
+    def dec_matrices():
+        dec_rows, dec_cols = slot_receivers(dec_slot[...], dec_recv[...], 16)
+        for h in range(5):
+            span = slice(h * 128, (h + 1) * 128)
+            dec_e[span, :] = ones_where(dec_cols[:, h : h + 1] == iota((128, G), 1))
+            dec_m[:, span] = ones_where(dec_rows[h : h + 1, :] == iota((G, 128), 0))
+        tab_t[...] = jnp.zeros((128, 128), F32)
+        for b in range(9):
+            tab_t[b : b + 1, 0:CD] = dec_send[b].astype(F32)
+        dec_tabs = jnp.transpose(tab_t[...]).astype(I32)
+        for b in range(9):
+            dec_g[b * CD : (b + 1) * CD, :] = ones_where(dec_tabs[0:CD, b : b + 1] == iota((CD, N), 1))
+        dec_in[9 * CD : 640, :] = jnp.zeros((64, L), BF)
+
+    for group in weight_copies[1:]:
+        for copy in group:
+            copy.start()
+    out_copy.start()
+    tab_copies[0].wait_recv()
+    tab_copies[1].wait_recv()
+    send_tab(tab_side.at[0, 1], tab_in.at[5], 5, (partner, c))
+    send_tab(tab_side.at[0, 2], tab_in.at[7], 7, (x_row, c))
+    send_tab(tab_side.at[1, 1], tab_in.at[6], 6, (partner, c))
+    send_tab(tab_side.at[1, 2], tab_in.at[8], 8, (x_row, c))
+    tab_in[0] = tab_out[0]
+    tab_in[2] = tab_side[0, 0]
+    tab_in[3] = tab_side[1, 0]
+    for piece, (first, count) in enumerate(GRID_PIECES):
+        arrived(0, enc_halo, 2, first, count, piece)
+        send(0, enc_halo, 2, 7, first, count, piece, (x_row, c), started)
+        arrived(0, enc_halo, 3, first, count, piece)
+        send(0, enc_halo, 3, 8, first, count, piece, (x_row, c), started)
     send(0, enc_halo, 2, 5, 0, G, 0, (partner, c), started)
-    arrived(0, enc_halo, 3, 0, G, 0)
     send(0, enc_halo, 3, 6, 0, G, 0, (partner, c), started)
-    weight_copies[0][2].wait()
-    weight_copies[0][3].wait()
+    tab_copies[2].wait_recv()
+    tab_copies[3].wait_recv()
+    near = (0, 1, 2, 3, 4)
+    tables(near, 0)
+    enc_matrices(near, 0)
+    for copy in weight_copies[0][1:]:
+        copy.wait()
+    arrived(0, enc_halo, 1, 0, G, 0)
+    arrived(0, enc_halo, 4, 0, G, 0)
+    messages(enc_halo, enc_w, CE, 0, near, msg)
     base[...] = dot(mesh_own[...], nf[0, 0])
-    arrived(0, enc_halo, 1, 0, G, 0)
-    messages(enc_halo, enc_w, CE, 0, (1, 2, 3), msg)
+    for copy in tab_copies[4:]:
+        copy.wait_recv()
+    diagonal = (5, 6, 7, 8)
+    tables(diagonal, 1)
+    enc_matrices(diagonal, 1)
+    arrived(0, enc_halo, 5, 0, G, 0)
+    arrived(0, enc_halo, 6, 0, G, 0)
+    messages(enc_halo, enc_w, CE, 0, (5, 6), msg)
+    agg[...] = dot(enc_m[:, 0 : 7 * CE], msg[0 : 7 * CE, :])
 
     proc_rows, proc_cols = slot_receivers(slot_pad[...], recv_pad[...], 24)
     for k in range(9):
-        at = iota((128, 2 * N), 1)
         for half in range(2):
-            receiver = pick(k, lambda b: proc_cols[:, 2 * b + half : 2 * b + half + 1])
-            receiver = jnp.where(receiver < 0, -1, receiver + N)
-            sender = tabs[:, 8 * k + 1 + half : 8 * k + 2 + half]
-            span = slice(half * 128, (half + 1) * 128)
-            proc_w[k, span, :] = ones_where((at == sender) | (at == receiver))
             receiver = pick(k, lambda b: proc_rows[2 * b + half : 2 * b + half + 1, :])
             first = k * CM + half * 128
             proc_m[:, first : first + 128] = ones_where(receiver == iota((N, 128), 0))
-
-    dec_rows, dec_cols = slot_receivers(dec_slot[...], dec_recv[...], 16)
-    for h in range(5):
-        span = slice(h * 128, (h + 1) * 128)
-        dec_e[span, :] = ones_where(dec_cols[:, h : h + 1] == iota((128, G), 1))
-        dec_m[:, span] = ones_where(dec_rows[h : h + 1, :] == iota((G, 128), 0))
-    tab_t[...] = jnp.zeros((128, 128), F32)
-    for b in range(9):
-        tab_t[b : b + 1, 0:CD] = dec_send[b].astype(F32)
-    dec_tabs = jnp.transpose(tab_t[...]).astype(I32)
-    for b in range(9):
-        dec_g[b * CD : (b + 1) * CD, :] = ones_where(dec_tabs[0:CD, b : b + 1] == iota((CD, N), 1))
-    dec_in[9 * CD : 640, :] = jnp.zeros((64, L), BF)
-
-    for k in (4, 5, 6):
-        arrived(0, enc_halo, k, 0, G, 0)
-    messages(enc_halo, enc_w, CE, 0, (4, 5, 6), msg)
-    agg[...] = dot(enc_m[:, 0 : 7 * CE], msg[0 : 7 * CE, :])
+    proc_matrices(near, 0)
+    dec_matrices()
+    for copy in far_copies:
+        copy.wait_recv()
+    found = []
+    for q in range(nc):
+        number = far_in[q]
+        device = number // CO
+        band = device // nc
+        index = (band % 2) * (nzx * CO) + (band // 2) * CO + number % CO
+        index = jnp.where(device % nc == c, index, -1)
+        found.append(
+            jnp.concatenate(
+                [ones_where(index == iota((FAR, 128), 1) + 128 * t) for t in range(max(1, nr * CO // 128))],
+                axis=1,
+            )
+        )
+    far_pick[...] = jnp.concatenate(found, axis=0)
+
     for k in (7, 8):
-        arrived(0, enc_halo, k, 0, G, 0)
+        for piece, (first, count) in enumerate(GRID_PIECES):
+            arrived(0, enc_halo, k, first, count, piece)
     messages(enc_halo, enc_w, CE, 0, (7, 8), msg)
-    summed = agg[...] + dot(enc_m[:, 7 * CE : 9 * CE], msg[7 * CE : 9 * CE, :])
-    lat[...] = node_update(0, mesh_own[...], summed, base[...])
+    ahead, pushes = finish_step(0, mesh_own[...], enc_m, 7 * CE, 9 * CE)
     for copy in started + tab_copies + far_copies:
         copy.wait_send()
 
     for s in range(2):
         i = s + 1
         halo = proc_halo.at[s]
-        for copy in weight_copies[i]:
-            copy.wait()
         own = lat[...]
-        sent = dot(own, ef[i, 0]).astype(BF)
-        halo[0, 0:N, :] = sent
-        place = pl.multiple_of((core * nzx + zx) * CO, CO)
-        gath[s, pl.ds(place, CO), :] = sent[0:CO, :]
-        peer_copies = []
-        for d in range(1, nzx):
-            copy = pltpu.make_async_remote_copy(
-                gath.at[s, pl.ds(place, CO)], gath.at[s, pl.ds(place, CO)],
-                g_ss.at[s, d], g_rs.at[s, d], device_id=peer(d), device_id_type=MESH,
-            )
-            copy.start()
-            peer_copies.append(copy)
-        started = []
-        for piece in range(4):
-            send(i, halo, 0, 3, piece * CH, CH, piece, (r, right), started)
-            send(i, halo, 0, 2, piece * CH, CH, piece, (r, left), started)
-            if piece == 0:
-                send(i, halo, 0, 4, 3 * CH, CH, 3, (x_row, c), started)
-                send(i, halo, 0, 4, 0, 3 * CH, 0, (x_row, c), started)
-                send(i, halo, 0, 1, 0, N, 0, (partner, c), started)
+        started, peer_copies = ahead, pushes
         receiver_part = dot(own, ef[i, 1]).astype(BF)
         for k in range(9):
             halo[k, N : 2 * N, :] = receiver_part
@@ -444,26 +565,8 @@
             device_id=(partner, c), device_id_type=MESH,
         )
         to_partner.start()
-        messages(halo, proc_w, CM, i, (2, 3), msg)
-
         to_partner.wait_recv()
-        if s == 0:
-            for copy in far_copies:
-                copy.wait_recv()
-        found = []
-        for q in range(nc):
-            number = far_in[q]
-            device = number // CO
-            band = device // nc
-            index = (band % 2) * (nzx * CO) + (band // 2) * CO + number % CO
-            index = jnp.where(device % nc == c, index, -1)
-            found.append(
-                jnp.concatenate(
-                    [ones_where(index == iota((FAR, 128), 1) + 128 * t) for t in range(max(1, nr * CO // 128))],
-                    axis=1,
-                )
-            )
-        chosen = dot(jnp.concatenate(found, axis=0), gath[s]).astype(BF)
+        chosen = dot(far_pick[...], gath[s]).astype(BF)
         c_out[s] = chosen
         mate_copies = []
         for q in range(1, nc):
@@ -474,6 +577,9 @@
             copy.start()
             mate_copies.append(copy)
 
+        messages(halo, proc_w, CM, i, (2, 3), msg)
+        if s == 0:
+            proc_matrices(diagonal, 1)
         arrived(i, halo, 4, 0, 3 * CH, 0)
         for k in (5, 6):
             arrived(i, halo, k, 0, N, 0)
@@ -488,8 +594,7 @@
             for piece in range(4):
                 arrived(i, halo, k, piece * CH, CH, piece)
         messages(halo, proc_w, CM, i, (7, 8), msg, pre)
-        summed = agg[...] + dot(proc_m[:, 7 * CM :], msg[7 * CM :, :])
-        lat[...] = node_update(i, own, summed, base[...])
+        ahead, pushes = finish_step(i, own, proc_m, 7 * CM, 9 * CM + FAR)
         for copy in started + peer_copies + mate_copies + [to_partner]:
             copy.wait_send()
 
@@ -526,9 +631,7 @@
 def on_device(nr, nc, *args):
     vmem = pl.BlockSpec(memory_space=pltpu.VMEM)
     hbm = pl.BlockSpec(memory_space=pl.ANY)
-    in_specs = [vmem] * 21
-    for at in (1, 5, 6, 8, 9, 11):
-        in_specs[at] = hbm
+    in_specs = [hbm] * 21
     args = list(args)
     args[4] = args[4].reshape(1, L)
     args[0] = args[0].T
@@ -543,6 +646,21 @@
         in_specs=in_specs,
         out_specs=vmem,
         scratch_shapes=[
+            pltpu.VMEM((9, 1, CE), I32),
+            pltpu.VMEM((9, 1, CM), I32),
+            pltpu.VMEM((CIN, G), BF),
+            pltpu.VMEM((CIN, L), BF),
+            pltpu.VMEM((L, L), BF),
+            pltpu.VMEM((1, L), F32),
+            pltpu.VMEM((1, EM), I32),
+            pltpu.VMEM((1, EM), I32),
+            pltpu.VMEM((1, EE), I32),
+            pltpu.VMEM((1, EE), I32),
+            pltpu.VMEM((4, L), F32),
+            pltpu.VMEM((4, L), F32),
+            pltpu.VMEM((9, 1, CD), I32),
+            pltpu.VMEM((1, ED), I32),
+            pltpu.VMEM((1, ED), I32),
             pltpu.VMEM((4, 2, L, L), BF),
             pltpu.VMEM((4, L, L), BF),
             pltpu.VMEM((4, 2, L, L), BF),
@@ -551,9 +669,12 @@
             pltpu.VMEM((CIN, L), BF),
             pltpu.VMEM((9, 8, 128), I32),
             pltpu.VMEM((9, 8, 128), I32),
+            pltpu.VMEM((2, 3, 8, 128), I32),
             pltpu.VMEM((128, 128), F32),
+            pltpu.VMEM((2, 128, 128), I32),
             pltpu.VMEM((FAR, 128), I32),
             pltpu.VMEM((nc, FAR, 128), I32),
+            pltpu.VMEM((nc * FAR, nr * CO), BF),
             pltpu.VMEM((1, EMP), I32),
             pltpu.VMEM((1, EMP), I32),
             pltpu.VMEM((16, 128), I32),
@@ -578,6 +699,7 @@
             pltpu.VMEM((N, L), F32),
             pltpu.VMEM((9 * CM + FAR, L), BF),
             dma((5, 4)),
+            dma((15,)),
             dma((9,)),
             dma((9,)),
             dma((nc,)),

time: 79.3 us -> 76.2 us (0.961)
  the two profiles are of different devices: /device:TPU:1 before, /device:TPU:64 now
where the time goes in v2:
time: 76.2 us; the launch traced here: 76.1 us
  Pallas kernels  74.5 us (98%)
  local copies, waits for them, and re-layouts  1.56 us (2%)
    pallas_call x1, Pallas kernels, on_device(): pl.pallas_call(functools.partial(body, nr, nc), out_shape=jax.ShapeDtypeS...  74.5 us
    unnamed x1, local copies, waits for them, and re-layouts  1.56 us

profile of v2, /device:TPU:64, one launch (start us, length us, event | category | flops | bytes accessed | tf_op | source)
XLA Modules:
  0.0 76.1 jit_solution(1301719456525642628)
XLA Ops:
  0.0 74.5 %shard_map.199 = f32[227,128]{1,0:T(8,128)} custom-call(bf16[227,128]{1,0:T(8,128)(2,1)} %bitcast.9, bf16[320,512]{1,0:T(8,128)(2,1)} %mesh_init.1, bf16[227,512]{1,0:T(8,128)(2,1)} %embed_first_any.1, bf16[512,512]{1,0:T(8,128)(2,1)} %embed_second_any.1, f32[1,512]{1,0:T(1,128)} %bitcast.13, bf16[4,2,512,512]{3,2,1,0:T(8,128)(2,1)} %edge_first_any.1, ...), custom_call_target="tpu_custom_call" | custom-call | tf_op jit(solution)/shard_map/pallas_call | solution.py:643
  74.6 1.6 %copy.23 = f32[128,227]{0,1:T(8,128)} copy(f32[128,227]{0,1:T(8,128)} %bitcast.7) | data formatting | bytes 232448

commit v3 on v2

--- a/solution.py
+++ b/solution.py
@@ -549,22 +549,18 @@
             send(i, halo, 2, 7, piece * CH, CH, piece, (x_row, c), started)
             arrived(i, halo, 3, piece * CH, CH, piece)
             send(i, halo, 3, 8, piece * CH, CH, piece, (x_row, c), started)
-            if piece == 0:
+            if piece == 1:
                 arrived(i, halo, 4, 3 * CH, CH, 3)
                 send(i, halo, 4, 8, 3 * CH, CH, 3, (r, right), started)
                 send(i, halo, 4, 7, 3 * CH, CH, 3, (r, left), started)
-        arrived(i, halo, 2, 3 * CH, CH, 3)
-        send(i, halo, 2, 5, 0, N, 0, (partner, c), started)
-        arrived(i, halo, 3, 3 * CH, CH, 3)
-        send(i, halo, 3, 6, 0, N, 0, (partner, c), started)
-        for copy in peer_copies:
-            copy.wait_recv()
-        mine = pl.ds(pl.multiple_of(core * (nzx * CO), CO), nzx * CO)
-        to_partner = pltpu.make_async_remote_copy(
-            gath.at[s, mine], gath.at[s, mine], p_ss.at[s], p_rs.at[s],
-            device_id=(partner, c), device_id_type=MESH,
-        )
-        to_partner.start()
+                for copy in peer_copies:
+                    copy.wait_recv()
+                mine = pl.ds(pl.multiple_of(core * (nzx * CO), CO), nzx * CO)
+                to_partner = pltpu.make_async_remote_copy(
+                    gath.at[s, mine], gath.at[s, mine], p_ss.at[s], p_rs.at[s],
+                    device_id=(partner, c), device_id_type=MESH,
+                )
+                to_partner.start()
         to_partner.wait_recv()
         chosen = dot(far_pick[...], gath[s]).astype(BF)
         c_out[s] = chosen
@@ -577,6 +573,10 @@
             copy.start()
             mate_copies.append(copy)
 
+        arrived(i, halo, 2, 3 * CH, CH, 3)
+        send(i, halo, 2, 5, 0, N, 0, (partner, c), started)
+        arrived(i, halo, 3, 3 * CH, CH, 3)
+        send(i, halo, 3, 6, 0, N, 0, (partner, c), started)
         messages(halo, proc_w, CM, i, (2, 3), msg)
         if s == 0:
             proc_matrices(diagonal, 1)

time: 76.2 us -> 73.9 us (0.970)
  Pallas kernels: 74.5 us -> 72.2 us
    pallas_call x1, Pallas kernels: 74.5 us -> 72.2 us  [on_device(): pl.pallas_call(functools.partial(body, nr, nc), out_shape=jax.ShapeDtypeS...]
where the time goes in v3:
time: 73.9 us; the launch traced here: 73.8 us
  Pallas kernels  72.2 us (98%)
  local copies, waits for them, and re-layouts  1.56 us (2%)
    pallas_call x1, Pallas kernels, on_device(): pl.pallas_call(functools.partial(body, nr, nc), out_shape=jax.ShapeDtypeS...  72.2 us
    unnamed x1, local copies, waits for them, and re-layouts  1.56 us

profile of v3, /device:TPU:64, one launch (start us, length us, event | category | flops | bytes accessed | tf_op | source)
XLA Modules:
  0.0 73.8 jit_solution(874541653982984758)
XLA Ops:
  0.0 72.2 %shard_map.199 = f32[227,128]{1,0:T(8,128)} custom-call(bf16[227,128]{1,0:T(8,128)(2,1)} %bitcast.9, bf16[320,512]{1,0:T(8,128)(2,1)} %mesh_init.1, bf16[227,512]{1,0:T(8,128)(2,1)} %embed_first_any.1, bf16[512,512]{1,0:T(8,128)(2,1)} %embed_second_any.1, f32[1,512]{1,0:T(1,128)} %bitcast.13, bf16[4,2,512,512]{3,2,1,0:T(8,128)(2,1)} %edge_first_any.1, ...), custom_call_target="tpu_custom_call" | custom-call | tf_op jit(solution)/shard_map/pallas_call | solution.py:643
  72.2 1.6 %copy.23 = f32[128,227]{0,1:T(8,128)} copy(f32[128,227]{0,1:T(8,128)} %bitcast.7) | data formatting | bytes 232448

commit v4 on v3

--- a/solution.py
+++ b/solution.py
@@ -603,7 +603,7 @@
     sent = dot(lat[...], ef[3, 0]).astype(BF)
     dec_out[...] = dot(dec_g[...], sent).astype(BF)
     dec_copies = []
-    for b in others:
+    for b in (0, 2, 6, 8, 1, 7, 3, 5):
         span = pl.ds(b * CD, CD)
         copy = pltpu.make_async_remote_copy(
             dec_out.at[span], dec_in.at[span], d_ss.at[b], d_rs.at[b],

time: 73.9 us -> 73.2 us (level)
  no operation moved by 1% of the time
where the time goes in v4:
time: 73.2 us; the launch traced here: 73.1 us
  Pallas kernels  71.5 us (98%)
  local copies, waits for them, and re-layouts  1.56 us (2%)
    pallas_call x1, Pallas kernels, on_device(): pl.pallas_call(functools.partial(body, nr, nc), out_shape=jax.ShapeDtypeS...  71.5 us
    unnamed x1, local copies, waits for them, and re-layouts  1.56 us

profile of v4, /device:TPU:64, one launch (start us, length us, event | category | flops | bytes accessed | tf_op | source)
XLA Modules:
  0.0 73.1 jit_solution(17769526803260607383)
XLA Ops:
  0.0 71.5 %shard_map.199 = f32[227,128]{1,0:T(8,128)} custom-call(bf16[227,128]{1,0:T(8,128)(2,1)} %bitcast.9, bf16[320,512]{1,0:T(8,128)(2,1)} %mesh_init.1, bf16[227,512]{1,0:T(8,128)(2,1)} %embed_first_any.1, bf16[512,512]{1,0:T(8,128)(2,1)} %embed_second_any.1, f32[1,512]{1,0:T(1,128)} %bitcast.13, bf16[4,2,512,512]{3,2,1,0:T(8,128)(2,1)} %edge_first_any.1, ...), custom_call_target="tpu_custom_call" | custom-call | tf_op jit(solution)/shard_map/pallas_call | solution.py:643
  71.5 1.6 %copy.23 = f32[128,227]{0,1:T(8,128)} copy(f32[128,227]{0,1:T(8,128)} %bitcast.7) | data formatting | bytes 232448
